TPU v7x, 256 devices: a whole 4x4x8 slice. The times are simulated.
256 devices in a mesh: depth: 32 (over x, y, core), tile: 8 (over z).
Axes of the slice: x: 4, y: 4, z: 8, core: 2. Of those that a mesh axis runs over, the one named last changes fastest.
Arguments:
- fronts: float32 [32, 8, 8, 2, 128, 128], P('depth', 'tile'), may hold values from -6 to 6
- probe_wave: float32 [2, 128, 128], replicated, may hold values from -6 to 6
- object_slices: bfloat16 [64, 2, 3072, 384], P('depth', None, 'tile')
- patch_list: int32 [35, 8, 3, 8], P(None, 'tile'), may hold values from 0 to 256, as said below
- counts: int32 [35, 8], P(None, 'tile'), may hold values from 1 to 8, as said below
Outputs:
- exit_waves: float32 [32, 8, 8, 2, 128, 128], P('depth', 'tile')
Inputs may be any that keep to these rules, and one draw needn't show every extreme that they name: `patch_list`: rows and columns of corners run from 0 to 256, and that end is reached. Among the live probes of one batch of one owner no tile is named more than 1 times; a batch of 8 probes names every tile exactly 1 times. `counts`: some batch of some owner holds 8 probes.
All inputs are finite; a program needn't handle non-finite values.
Results may differ from a plain program's by a relative error of at most 0.0003.
Values may be sent and summed in bfloat16 or wider, within the bound.
A program may use at most 64 MiB of HBM per device.

v0:
```python
import math
import jax
import jax.numpy as jnp
from jax import lax
from jax.sharding import PartitionSpec as P

STEPS = 4
fresnel_rate = 0.3


def from_behind(value, axis, steps):
    count = lax.axis_size(axis)
    leading, last = (max(0, -steps), min(count, count - steps))
    return lax.ppermute(value, axis, [(source, source + steps) for source in range(leading, last)])


def dft_tables(width, inverse):
    index = jnp.arange(width, dtype=jnp.int32)
    angle = 2.0 * math.pi / width * (index[:, None] * index[None, :] % width).astype(jnp.float32)
    cosine = jnp.cos(angle)
    sine = jnp.sin(angle)
    if inverse:
        cosine = cosine / width
        imagine = sine / width
    else:
        imagine = -sine
    return (cosine, cosine + imagine, imagine - cosine)


def plane_dot(plane, table):
    shape = plane.shape
    flat = plane.reshape(-1, shape[-1])
    return jnp.dot(
        flat, table, precision=lax.Precision.HIGHEST, preferred_element_type=jnp.float32
    ).reshape(shape)


def right_multiply(real_part, imag_part, tables):
    cosine, summed, differ = tables
    first = plane_dot(real_part + imag_part, cosine)
    second = plane_dot(real_part, differ)
    third = plane_dot(imag_part, summed)
    return (first - third, first + second)


def transform(real_part, imag_part, tables):
    real_part, imag_part = right_multiply(real_part, imag_part, tables)
    return right_multiply(jnp.swapaxes(real_part, -1, -2), jnp.swapaxes(imag_part, -1, -2), tables)


def fresnel(width):
    index = jnp.arange(width, dtype=jnp.int32)
    freq = jnp.where(index < width // 2, index, index - width).astype(jnp.float32)
    phase = -2.0 * math.pi * fresnel_rate / width * (freq[:, None] ** 2 + freq[None, :] ** 2)
    return (jnp.cos(phase), jnp.sin(phase))


def slab_pass(wavefield, patches):
    width = wavefield.shape[-1]
    forward = dft_tables(width, False)
    backward = dft_tables(width, True)
    kernel_cos, kernel_sin = fresnel(width)
    real_part = wavefield[:, 0]
    imag_part = wavefield[:, 1]
    for layer in range(2):
        trans_real = patches[:, layer, 0].astype(jnp.float32)
        trans_imag = patches[:, layer, 1].astype(jnp.float32)
        real_part, imag_part = (
            real_part * trans_real - imag_part * trans_imag,
            real_part * trans_imag + imag_part * trans_real,
        )
        spec_real, spec_imag = transform(real_part, imag_part, forward)
        spec_real, spec_imag = (
            spec_real * kernel_cos - spec_imag * kernel_sin,
            spec_real * kernel_sin + spec_imag * kernel_cos,
        )
        real_part, imag_part = transform(spec_real, spec_imag, backward)
    return jnp.stack([real_part, imag_part], axis=1)


def rank_within(tile_ids, live):
    slot_index = jnp.arange(tile_ids.shape[0], dtype=jnp.int32)
    same = (
        (tile_ids[:, None] == tile_ids[None, :])
        & live[None, :]
        & (slot_index[None, :] < slot_index[:, None])
    )
    return jnp.sum(same.astype(jnp.int32), axis=1)


def cut_from(source, row_value, column_value, width):
    zero = jnp.zeros((), jnp.int32)
    return lax.dynamic_slice(source, (zero, zero, row_value, column_value), (2, 2, width, width))


def per_device(fronts, probe_wave, object_slices, patch_list, counts):
    depth_count = lax.axis_size("depth")
    tile_count = lax.axis_size("tile")
    depth_index = lax.axis_index("depth")
    tile_index = lax.axis_index("tile")
    slots = fronts.shape[2]
    width = fronts.shape[-1]
    pair = slots // tile_count
    slot_index = jnp.arange(slots, dtype=jnp.int32)
    own_lists = patch_list[:, 0]
    own_counts = counts[:, 0]
    batch_ids = [step + depth_count - 1 - depth_index for step in range(STEPS)]
    step_lists = jnp.stack(
        [lax.dynamic_index_in_dim(own_lists, batch, 0, keepdims=False) for batch in batch_ids]
    )
    step_counts = jnp.stack(
        [lax.dynamic_index_in_dim(own_counts, batch, 0, keepdims=False) for batch in batch_ids]
    )

    def outgoing(all_lists, all_counts):
        tile_ids = all_lists[:, 0]
        live = slot_index[None, :] < all_counts[:, None]
        order = jax.vmap(rank_within)(tile_ids, live)
        target = live & (tile_ids == tile_index)
        choose = (
            target[:, None, :]
            & (order[:, None, :] == jnp.arange(pair, dtype=jnp.int32)[None, :, None])
        ).astype(jnp.int32)
        row_start = jnp.sum(choose * all_lists[:, 1][:, None, :], axis=-1)
        column_start = jnp.sum(choose * all_lists[:, 2][:, None, :], axis=-1)
        valid = jnp.sum(choose, axis=-1) > 0

        def cut_local(row_value, column_value):
            return cut_from(object_slices, row_value, column_value, width)

        cuts = jax.vmap(jax.vmap(cut_local))(row_start, column_start)
        return jnp.where(valid[:, :, None, None, None, None], cuts, jnp.zeros_like(cuts))

    wavefield = fronts[0, 0]
    for step in range(STEPS):
        listing = step_lists[step]
        count = step_counts[step]
        live = (slot_index < count).astype(jnp.float32)[:, None, None, None]
        if step > 0:
            arrived = from_behind(wavefield, "depth", 1)
            wavefield = jnp.where(depth_index == 0, probe_wave[None] * live, arrived)
        else:
            wavefield = wavefield * live
        got_lists, got_counts = (
            lax.all_gather(listing[None], "tile", axis=0, tiled=True),
            lax.all_gather(count[None], "tile", axis=0, tiled=True),
        )
        received = lax.all_to_all(
            outgoing(got_lists, got_counts), "tile", split_axis=0, concat_axis=0, tiled=True
        )
        incoming_tile_ids = listing[0]
        incoming_live = slot_index < count
        incoming_order = rank_within(incoming_tile_ids, incoming_live)
        place = incoming_tile_ids * pair + jnp.minimum(incoming_order, pair - 1)
        flat = received.reshape((tile_count * pair,) + received.shape[2:])
        patches = jnp.take(flat, place, axis=0)
        wavefield = slab_pass(wavefield, patches)
    return wavefield[None, None]


def solution(mesh):
    in_specs = (
        P("depth", "tile", None, None, None, None),
        P(),
        P("depth", None, "tile", None),
        P(None, "tile", None, None),
        P(None, "tile"),
    )
    out_specs = P("depth", "tile", None, None, None, None)
    return jax.shard_map(
        per_device, mesh=mesh, in_specs=in_specs, out_specs=out_specs, check_vma=False
    )
```

profile of v0, /device:TPU:38, one launch (start us, length us, event | category | flops | bytes accessed | tf_op | source)
XLA Modules:
  0.0 397.6 jit_solution(2629929279038056412)
XLA Ops:
  7.9 15.2 %all-reduce.4 = (s32[8]{0:T(128)S(1)}, s32[8]{0:T(128)S(1)}, s32[8]{0:T(128)S(1)}, s32[8]{0:T(128)S(1)}) all-reduce(s32[8]{0:T(128)S(1)} %bitcast_dynamic-update-slice_fusion.4, s32[8]{0:T(128)S(1)} %bitcast_dynamic-update-slice_fusion.5, s32[8]{0:T(128)S(1)} %bitcast_dynamic-update-slice_fusion.6, ...), channel_id=8, replica_groups=mesh['depth'=32,'tile'=8] {'tile'}, use_global_device_ids=true, to_apply=%add.3 | all-reduce | flops 32 | bytes 256 | tf_op jit(solution)/shard_map/all_gather | solution.py:146
  24.5 20.8 %all-gather.7 = s32[8,1,3,8]{3,1,2,0:T(1,128)S(1)} all-gather(s32[1,1,3,8]{3,1,2,0:T(1,128)S(1)} %copy.293), channel_id=9, replica_groups=mesh['depth'=32,'tile'=8] {'tile'}, dimensions={0}, use_global_device_ids=true | all-gather | bytes 864 | tf_op jit(solution)/shard_map/all_gather | solution.py:145
  45.4 20.7 %all-gather.5 = s32[8,1,3,8]{3,1,2,0:T(1,128)S(1)} all-gather(s32[1,1,3,8]{3,1,2,0:T(1,128)S(1)} %copy.292), channel_id=7, replica_groups=mesh['depth'=32,'tile'=8] {'tile'}, dimensions={0}, use_global_device_ids=true | all-gather | bytes 864 | tf_op jit(solution)/shard_map/all_gather | solution.py:145
  66.2 20.7 %all-gather.3 = s32[8,1,3,8]{3,1,2,0:T(1,128)S(1)} all-gather(s32[1,1,3,8]{3,1,2,0:T(1,128)S(1)} %copy.291), channel_id=5, replica_groups=mesh['depth'=32,'tile'=8] {'tile'}, dimensions={0}, use_global_device_ids=true | all-gather | bytes 864 | tf_op jit(solution)/shard_map/all_gather | solution.py:145
  87.0 21.1 %all-gather.1 = s32[8,1,3,8]{3,1,2,0:T(1,128)S(1)} all-gather(s32[1,1,3,8]{3,1,2,0:T(1,128)S(1)} %copy.290), channel_id=3, replica_groups=mesh['depth'=32,'tile'=8] {'tile'}, dimensions={0}, use_global_device_ids=true | all-gather | bytes 864 | tf_op jit(solution)/shard_map/all_gather | solution.py:145
  110.1 24.6 %while.4 = (s32[]{:T(128)}, bf16[2,2,384,384]{3,2,1,0:T(8,128)(2,1)}, s32[8,4]{0,1:T(4,128)S(1)}, bf16[8,2,2,128,128]{4,3,2,1,0:T(8,128)(2,1)S(1)}, s32[]{:T(128)}) while((s32[]{:T(128)}, bf16[2,2,384,384]{3,2,1,0:T(8,128)(2,1)}, s32[8,4]{0,1:T(4,128)S(1)}, bf16[8,2,2,128,128]{4,3,2,1,0:T(8,128)(2,1)S(1)}, s32[]{:T(128)}) %tuple.93), condition=%wide.while_cond, body=%wide.while_body.sunk | while | flops 2 | bytes 262269 | solution.py:93
  110.8 2.4 bitcast_dynamic-update-slice_fusion.12
  113.9 2.4 bitcast_dynamic-update-slice_fusion.12
  116.9 2.4 bitcast_dynamic-update-slice_fusion.12
  120.0 2.4 bitcast_dynamic-update-slice_fusion.12
  123.1 2.4 bitcast_dynamic-update-slice_fusion.12
  126.2 2.4 bitcast_dynamic-update-slice_fusion.12
  129.2 2.4 bitcast_dynamic-update-slice_fusion.12
  132.3 2.4 bitcast_dynamic-update-slice_fusion.12
  135.9 6.2 %all-to-all-start = ((bf16[8,1,2,2,128,128]{5,4,3,2,1,0:T(8,128)(2,1)}), bf16[8,1,2,2,128,128]{5,4,3,2,1,0:T(8,128)(2,1)S(1)}, u32[]{:S(2)}, u32[]{:S(2)}) async-start(bf16[8,1,2,2,128,128]{5,4,3,2,1,0:T(8,128)(2,1)} %bitcast_select_fusion.3), calls=%async_computation | async-start | bytes 2097152 | tf_op jit(solution)/shard_map/all_to_all | solution.py:148
  145.4 24.1 %while.5 = (s32[]{:T(128)}, bf16[2,2,384,384]{3,2,1,0:T(8,128)(2,1)}, s32[8,4]{0,1:T(4,128)S(1)}, bf16[8,2,2,128,128]{4,3,2,1,0:T(8,128)(2,1)S(1)}, s32[]{:T(128)}) while((s32[]{:T(128)}, bf16[2,2,384,384]{3,2,1,0:T(8,128)(2,1)}, s32[8,4]{0,1:T(4,128)S(1)}, bf16[8,2,2,128,128]{4,3,2,1,0:T(8,128)(2,1)S(1)}, s32[]{:T(128)}) %tuple.105), condition=%wide.while_cond.1, body=%wide.while_body.1.sunk | while | flops 2 | bytes 262269 | solution.py:93
  171.6 29.4 %while.6 = (s32[]{:T(128)}, bf16[2,2,384,384]{3,2,1,0:T(8,128)(2,1)}, s32[8,4]{0,1:T(4,128)S(1)}, bf16[8,2,2,128,128]{4,3,2,1,0:T(8,128)(2,1)}, s32[]{:T(128)}) while((s32[]{:T(128)}, bf16[2,2,384,384]{3,2,1,0:T(8,128)(2,1)}, s32[8,4]{0,1:T(4,128)S(1)}, bf16[8,2,2,128,128]{4,3,2,1,0:T(8,128)(2,1)}, s32[]{:T(128)}) %tuple.106), condition=%wide.while_cond.2, body=%wide.while_body.2.sunk | while | flops 2 | bytes 263793 | solution.py:93
  172.2 3.0 bitcast_dynamic-update-slice_fusion.14
  175.9 3.0 bitcast_dynamic-update-slice_fusion.14
  179.6 3.0 bitcast_dynamic-update-slice_fusion.14
  183.3 3.0 bitcast_dynamic-update-slice_fusion.14
  186.9 3.0 bitcast_dynamic-update-slice_fusion.14
  190.6 3.0 bitcast_dynamic-update-slice_fusion.14
  194.3 3.0 bitcast_dynamic-update-slice_fusion.14
  198.0 3.0 bitcast_dynamic-update-slice_fusion.14
  203.8 23.7 %while.7 = (s32[]{:T(128)}, bf16[2,2,384,384]{3,2,1,0:T(8,128)(2,1)}, s32[8,4]{0,1:T(4,128)S(1)}, bf16[8,2,2,128,128]{4,3,2,1,0:T(8,128)(2,1)S(1)}, s32[]{:T(128)}) while((s32[]{:T(128)}, bf16[2,2,384,384]{3,2,1,0:T(8,128)(2,1)}, s32[8,4]{0,1:T(4,128)S(1)}, bf16[8,2,2,128,128]{4,3,2,1,0:T(8,128)(2,1)S(1)}, s32[]{:T(128)}) %tuple.107), condition=%wide.while_cond.3, body=%wide.while_body.3.sunk | while | flops 2 | bytes 262269 | solution.py:93
  227.5 7.4 %all-to-all-start.1 = ((bf16[8,1,2,2,128,128]{5,4,3,2,1,0:T(8,128)(2,1)}), bf16[8,1,2,2,128,128]{5,4,3,2,1,0:T(8,128)(2,1)}, u32[]{:S(2)}, u32[]{:S(2)}) async-start(bf16[8,1,2,2,128,128]{5,4,3,2,1,0:T(8,128)(2,1)} %bitcast_select_fusion.2), calls=%async_computation.1 | async-start | bytes 2097152 | tf_op jit(solution)/shard_map/all_to_all | solution.py:148
  266.0 7.2 %all-to-all-start.2 = ((bf16[8,1,2,2,128,128]{5,4,3,2,1,0:T(8,128)(2,1)}), bf16[8,1,2,2,128,128]{5,4,3,2,1,0:T(8,128)(2,1)S(1)}, u32[]{:S(2)}, u32[]{:S(2)}) async-start(bf16[8,1,2,2,128,128]{5,4,3,2,1,0:T(8,128)(2,1)} %bitcast_select_fusion.1), calls=%async_computation.2 | async-start | bytes 2097152 | tf_op jit(solution)/shard_map/all_to_all | solution.py:148
  275.3 4.0 %collective-permute-done = f32[8,2,128,128]{3,2,0,1:T(8,128)} collective-permute-done((f32[8,2,128,128]{3,2,0,1:T(8,128)S(1)}, f32[8,2,128,128]{3,2,0,1:T(8,128)}, u32[]{:S(2)}, u32[]{:S(2)}) %collective-permute-start) | collective-permute-done | bytes 1048608 | tf_op jit(solution)/shard_map/ppermute | solution.py:14
  310.8 7.2 %all-to-all-start.3 = ((bf16[8,1,2,2,128,128]{5,4,3,2,1,0:T(8,128)(2,1)}), bf16[8,1,2,2,128,128]{5,4,3,2,1,0:T(8,128)(2,1)S(1)}, u32[]{:S(2)}, u32[]{:S(2)}) async-start(bf16[8,1,2,2,128,128]{5,4,3,2,1,0:T(8,128)(2,1)} %bitcast_select_fusion), calls=%async_computation.3 | async-start | bytes 2097152 | tf_op jit(solution)/shard_map/all_to_all | solution.py:148
  318.9 6.5 %collective-permute-done.1 = f32[8,2,128,128]{3,2,0,1:T(8,128)} collective-permute-done((f32[8,2,128,128]{3,2,0,1:T(8,128)}, f32[8,2,128,128]{3,2,0,1:T(8,128)}, u32[]{:S(2)}, u32[]{:S(2)}) %collective-permute-start.1) | collective-permute-done | bytes 1048608 | tf_op jit(solution)/shard_map/ppermute | solution.py:14
  356.6 14.8 %collective-permute-done.2 = f32[8,2,128,128]{3,2,0,1:T(8,128)S(1)} collective-permute-done((f32[8,2,128,128]{3,2,0,1:T(8,128)}, f32[8,2,128,128]{3,2,0,1:T(8,128)S(1)}, u32[]{:S(2)}, u32[]{:S(2)}) %collective-permute-start.2) | collective-permute-done | bytes 1048608 | tf_op jit(solution)/shard_map/ppermute | solution.py:14
  (282 shorter events, 200.5 us)
Async XLA Ops:
  135.9 91.7 %all-to-all-start = ((bf16[8,1,2,2,128,128]{5,4,3,2,1,0:T(8,128)(2,1)}), bf16[8,1,2,2,128,128]{5,4,3,2,1,0:T(8,128)(2,1)S(1)}, u32[]{:S(2)}, u32[]{:S(2)}) async-start(bf16[8,1,2,2,128,128]{5,4,3,2,1,0:T(8,128)(2,1)} %bitcast_select_fusion.3), calls=%async_computation | async-start | bytes 2097152 | tf_op jit(solution)/shard_map/all_to_all | solution.py:148
  227.5 7.4 %copy-start = (bf16[8,2,2,128,128]{4,3,2,1,0:T(8,128)(2,1)}, bf16[8,2,2,128,128]{4,3,2,1,0:T(8,128)(2,1)S(1)}, u32[]{:S(2)}) copy-start(bf16[8,2,2,128,128]{4,3,2,1,0:T(8,128)(2,1)S(1)} %get-tuple-element.37) | copy-start | bytes 3145732
  227.5 38.4 %all-to-all-start.1 = ((bf16[8,1,2,2,128,128]{5,4,3,2,1,0:T(8,128)(2,1)}), bf16[8,1,2,2,128,128]{5,4,3,2,1,0:T(8,128)(2,1)}, u32[]{:S(2)}, u32[]{:S(2)}) async-start(bf16[8,1,2,2,128,128]{5,4,3,2,1,0:T(8,128)(2,1)} %bitcast_select_fusion.2), calls=%async_computation.1 | async-start | bytes 2097152 | tf_op jit(solution)/shard_map/all_to_all | solution.py:148
  261.0 18.3 %collective-permute-start = (f32[8,2,128,128]{3,2,0,1:T(8,128)S(1)}, f32[8,2,128,128]{3,2,0,1:T(8,128)}, u32[]{:S(2)}, u32[]{:S(2)}) collective-permute-start(f32[8,2,128,128]{3,2,0,1:T(8,128)S(1)} %pad_maximum_fusion), channel_id=1, source_target_pairs={{0,8},{8,16},{16,24},{24,32},{32,40},{40,48},{48,56},{56,64},{64,7... | collective-permute-start | bytes 3145736 | tf_op jit(solution)/shard_map/ppermute | solution.py:14
  266.0 44.8 %all-to-all-start.2 = ((bf16[8,1,2,2,128,128]{5,4,3,2,1,0:T(8,128)(2,1)}), bf16[8,1,2,2,128,128]{5,4,3,2,1,0:T(8,128)(2,1)S(1)}, u32[]{:S(2)}, u32[]{:S(2)}) async-start(bf16[8,1,2,2,128,128]{5,4,3,2,1,0:T(8,128)(2,1)} %bitcast_select_fusion.1), calls=%async_computation.2 | async-start | bytes 2097152 | tf_op jit(solution)/shard_map/all_to_all | solution.py:148
  275.1 4.2 %copy-start.2 = (f32[2,128,128]{2,1,0:T(8,128)S(1)}, f32[2,128,128]{2,1,0:T(8,128)}, u32[]{:S(2)}) copy-start(f32[2,128,128]{2,1,0:T(8,128)} %param.8) | copy-start | bytes 393220
  305.9 3.8 copy-start.1
  306.9 18.5 %collective-permute-start.1 = (f32[8,2,128,128]{3,2,0,1:T(8,128)}, f32[8,2,128,128]{3,2,0,1:T(8,128)}, u32[]{:S(2)}, u32[]{:S(2)}) collective-permute-start(f32[8,2,128,128]{3,2,0,1:T(8,128)} %pad_maximum_fusion.1), channel_id=1, source_target_pairs={{0,8},{8,16},{16,24},{24,32},{32,40},{40,48},{48,56},{56,64},{64,7... | collective-permute-start | bytes 3145736 | tf_op jit(solution)/shard_map/ppermute | solution.py:14
  310.8 44.9 %all-to-all-start.3 = ((bf16[8,1,2,2,128,128]{5,4,3,2,1,0:T(8,128)(2,1)}), bf16[8,1,2,2,128,128]{5,4,3,2,1,0:T(8,128)(2,1)S(1)}, u32[]{:S(2)}, u32[]{:S(2)}) async-start(bf16[8,1,2,2,128,128]{5,4,3,2,1,0:T(8,128)(2,1)} %bitcast_select_fusion), calls=%async_computation.3 | async-start | bytes 2097152 | tf_op jit(solution)/shard_map/all_to_all | solution.py:148
  352.9 18.4 %collective-permute-start.2 = (f32[8,2,128,128]{3,2,0,1:T(8,128)}, f32[8,2,128,128]{3,2,0,1:T(8,128)S(1)}, u32[]{:S(2)}, u32[]{:S(2)}) collective-permute-start(f32[8,2,128,128]{3,2,0,1:T(8,128)} %pad_maximum_fusion.2), channel_id=1, source_target_pairs={{0,8},{8,16},{16,24},{24,32},{32,40},{40,48},{48,56},{56,64},{64,7... | collective-permute-start | bytes 3145736 | tf_op jit(solution)/shard_map/ppermute | solution.py:14
where the time goes:
time: 404 us; the launch traced here: 398 us
  local copies, waits for them, and re-layouts  118 us (29%)
  matrix products  99.2 us (25%)
  blocking collectives  98.6 us (24%)
  starting transfers between devices  33.7 us (8%)
  waiting for transfers between devices  25.3 us (6%)
  other arithmetic  21 us (5%)
    gather x96, local copies, waits for them, and re-layouts  101 us
    dot_general x96, matrix products, plane_dot(): jnp.dot(flat, table, precision=lax.Precision.HIGHEST, preferred_element_t...  99.2 us
    all_gather x4, blocking collectives, per_device(): lax.all_gather(listing[None], 'tile', axis=0, tiled=True)  83.4 us
    all_to_all x4, starting transfers between devices, per_device(): lax.all_to_all(outgoing(got_lists, got_counts), 'tile', split_axis=0, con...  28 us
    ppermute x3, waiting for transfers between devices, from_behind(): lax.ppermute(value, axis, [(source, source + steps) for source in range(l...  25.3 us
    all_gather x1, blocking collectives, per_device(): lax.all_gather(count[None], 'tile', axis=0, tiled=True)  15.2 us
    unnamed x23, local copies, waits for them, and re-layouts  8.72 us
  transfers between devices with their start and end apart: 7, of which 3 were waited for; matrix products, arithmetic and copies ran while one was open for 44% of the time, Pallas kernels for 0%

commit v1 on v0

--- a/solution.py
+++ b/solution.py
@@ -143,7 +143,10 @@
             wavefield = wavefield * live
         got_lists, got_counts = (
             lax.all_gather(listing[None], "tile", axis=0, tiled=True),
-            lax.all_gather(count[None], "tile", axis=0, tiled=True),
+            jnp.concatenate(
+                lax.all_to_all(jnp.stack([count[None]] * lax.axis_size("tile")), "tile", 0, 0),
+                axis=0,
+            ),
         )
         received = lax.all_to_all(
             outgoing(got_lists, got_counts), "tile", split_axis=0, concat_axis=0, tiled=True

time: 404 us -> 417 us (1.032)
  starting transfers between devices: 33.7 us -> 57.8 us
  blocking collectives: 98.6 us -> 85.2 us
  waiting for transfers between devices: 25.3 us -> 32.5 us
  local copies, waits for them, and re-layouts: 118 us -> 111 us
    all_to_all x0 -> x4, starting transfers between devices: none -> 24.2 us  [per_device(): lax.all_to_all(jnp.stack([count[None]] * lax.axis_size('tile')), 'tile',...]
    all_to_all x0 -> x4, waiting for transfers between devices: none -> 17.6 us  [per_device(): lax.all_to_all(jnp.stack([count[None]] * lax.axis_size('tile')), 'tile',...]
    all_gather x1 -> x0, blocking collectives: 15.2 us -> none  [per_device(): lax.all_gather(count[None], 'tile', axis=0, tiled=True)]
    ppermute x3, waiting for transfers between devices: 25.3 us -> 14.9 us  [from_behind(): lax.ppermute(value, axis, [(source, source + steps) for source in range(l...]
    unnamed x23 -> x12, local copies, waits for them, and re-layouts: 8.72 us -> 2 us
    gather x96, local copies, waits for them, and re-layouts: 101 us -> 96.6 us
    another operation x1 -> x5, local copies, waits for them, and re-layouts: 0.01 us -> 4.78 us  [the longest x4 4.78 us: per_device(): jnp.stack([count[None]] * lax.axis_size('tile'))]
  transfers between devices with their start and end apart: 7 -> 11, of which waited for: 3 -> 4; matrix products, arithmetic and copies ran while one was open for 44% -> 42% of each run, Pallas kernels for 0% -> 0%
where the time goes in v1:
time: 417 us; the launch traced here: 411 us
  local copies, waits for them, and re-layouts  111 us (27%)
  matrix products  99.1 us (24%)
  blocking collectives  85.2 us (20%)
  starting transfers between devices  57.8 us (14%)
  waiting for transfers between devices  32.5 us (8%)
  other arithmetic  22.9 us (5%)
    dot_general x96, matrix products, plane_dot(): jnp.dot(flat, table, precision=lax.Precision.HIGHEST, preferred_element_t...  99.1 us
    gather x96, local copies, waits for them, and re-layouts  96.6 us
    all_gather x4, blocking collectives, per_device(): lax.all_gather(listing[None], 'tile', axis=0, tiled=True)  85.2 us
    all_to_all x4, starting transfers between devices, per_device(): lax.all_to_all(outgoing(got_lists, got_counts), 'tile', split_axis=0, con...  26.7 us
    all_to_all x4, starting transfers between devices, per_device(): lax.all_to_all(jnp.stack([count[None]] * lax.axis_size('tile')), 'tile',...  24.2 us
    all_to_all x4, waiting for transfers between devices, per_device(): lax.all_to_all(jnp.stack([count[None]] * lax.axis_size('tile')), 'tile',...  17.6 us
    ppermute x3, waiting for transfers between devices, from_behind(): lax.ppermute(value, axis, [(source, source + steps) for source in range(l...  14.9 us
  transfers between devices with their start and end apart: 11, of which 4 were waited for; matrix products, arithmetic and copies ran while one was open for 42% of the time, Pallas kernels for 0%

profile of v1, /device:TPU:38, one launch (start us, length us, event | category | flops | bytes accessed | tf_op | source)
XLA Modules:
  0.0 410.5 jit_solution(9118509250556246812)
XLA Ops:
  2.6 8.6 %all-to-all-start.6 = ((s32[8,1,1]{2,1,0:T(1,128)}), s32[8,1,1]{2,1,0:T(1,128)S(1)}, u32[]{:S(2)}, u32[]{:S(2)}) async-start(s32[8,1,1]{2,1,0:T(1,128)} %stack.64), calls=%async_computation.6 | async-start | bytes 8192 | tf_op jit(solution)/shard_map/all_to_all | solution.py:147
  12.2 22.1 %all-gather = s32[8,1,3,8]{3,1,2,0:T(1,128)S(1)} all-gather(s32[1,1,3,8]{3,1,2,0:T(1,128)S(1)} %copy.352), channel_id=2, replica_groups=mesh['depth'=32,'tile'=8] {'tile'}, dimensions={0}, use_global_device_ids=true | all-gather | bytes 864 | tf_op jit(solution)/shard_map/all_gather | solution.py:145
  35.6 21.0 %all-gather.1 = s32[8,1,3,8]{3,1,2,0:T(1,128)S(1)} all-gather(s32[1,1,3,8]{3,1,2,0:T(1,128)S(1)} %copy.353), channel_id=3, replica_groups=mesh['depth'=32,'tile'=8] {'tile'}, dimensions={0}, use_global_device_ids=true | all-gather | bytes 864 | tf_op jit(solution)/shard_map/all_gather | solution.py:145
  58.0 21.2 %all-gather.2 = s32[8,1,3,8]{3,1,2,0:T(1,128)S(1)} all-gather(s32[1,1,3,8]{3,1,2,0:T(1,128)S(1)} %copy.354), channel_id=4, replica_groups=mesh['depth'=32,'tile'=8] {'tile'}, dimensions={0}, use_global_device_ids=true | all-gather | bytes 864 | tf_op jit(solution)/shard_map/all_gather | solution.py:145
  81.1 21.0 %all-gather.3 = s32[8,1,3,8]{3,1,2,0:T(1,128)S(1)} all-gather(s32[1,1,3,8]{3,1,2,0:T(1,128)S(1)} %copy.355), channel_id=5, replica_groups=mesh['depth'=32,'tile'=8] {'tile'}, dimensions={0}, use_global_device_ids=true | all-gather | bytes 864 | tf_op jit(solution)/shard_map/all_gather | solution.py:145
  105.7 6.3 %all-to-all-start.4 = ((s32[8,1,1]{2,1,0:T(1,128)}), s32[8,1,1]{2,1,0:T(1,128)S(1)}, u32[]{:S(2)}, u32[]{:S(2)}) async-start(s32[8,1,1]{2,1,0:T(1,128)} %stack.60), calls=%async_computation.4 | async-start | bytes 8192 | tf_op jit(solution)/shard_map/all_to_all | solution.py:147
  112.3 5.8 %all-to-all-done.4 = s32[8,1,1]{2,1,0:T(1,128)S(1)} async-done(((s32[8,1,1]{2,1,0:T(1,128)}), s32[8,1,1]{2,1,0:T(1,128)S(1)}, u32[]{:S(2)}, u32[]{:S(2)}) %all-to-all-start.4) | async-done | bytes 64 | tf_op jit(solution)/shard_map/all_to_all | solution.py:147
  119.4 4.7 %all-to-all-start.2 = ((s32[8,1,1]{2,1,0:T(1,128)}), s32[8,1,1]{2,1,0:T(1,128)S(1)}, u32[]{:S(2)}, u32[]{:S(2)}) async-start(s32[8,1,1]{2,1,0:T(1,128)} %stack.56), calls=%async_computation.2 | async-start | bytes 8192 | tf_op jit(solution)/shard_map/all_to_all | solution.py:147
  124.4 5.9 %all-to-all-done.2 = s32[8,1,1]{2,1,0:T(1,128)S(1)} async-done(((s32[8,1,1]{2,1,0:T(1,128)}), s32[8,1,1]{2,1,0:T(1,128)S(1)}, u32[]{:S(2)}, u32[]{:S(2)}) %all-to-all-start.2) | async-done | bytes 64 | tf_op jit(solution)/shard_map/all_to_all | solution.py:147
  131.5 4.7 %all-to-all-start = ((s32[8,1,1]{2,1,0:T(1,128)}), s32[8,1,1]{2,1,0:T(1,128)S(1)}, u32[]{:S(2)}, u32[]{:S(2)}) async-start(s32[8,1,1]{2,1,0:T(1,128)} %stack.52), calls=%async_computation | async-start | bytes 8192 | tf_op jit(solution)/shard_map/all_to_all | solution.py:147
  136.4 5.9 %all-to-all-done = s32[8,1,1]{2,1,0:T(1,128)S(1)} async-done(((s32[8,1,1]{2,1,0:T(1,128)}), s32[8,1,1]{2,1,0:T(1,128)S(1)}, u32[]{:S(2)}, u32[]{:S(2)}) %all-to-all-start) | async-done | bytes 64 | tf_op jit(solution)/shard_map/all_to_all | solution.py:147
  144.5 24.7 %while.4 = (s32[]{:T(128)}, bf16[2,2,384,384]{3,2,1,0:T(8,128)(2,1)}, s32[8,4]{0,1:T(4,128)S(1)}, bf16[8,2,2,128,128]{4,3,2,1,0:T(8,128)(2,1)S(1)}, s32[]{:T(128)}) while((s32[]{:T(128)}, bf16[2,2,384,384]{3,2,1,0:T(8,128)(2,1)}, s32[8,4]{0,1:T(4,128)S(1)}, bf16[8,2,2,128,128]{4,3,2,1,0:T(8,128)(2,1)S(1)}, s32[]{:T(128)}) %tuple.93), condition=%wide.while_cond, body=%wide.while_body.sunk | while | flops 2 | bytes 262269 | solution.py:93
  145.2 2.4 bitcast_dynamic-update-slice_fusion.8
  148.3 2.4 bitcast_dynamic-update-slice_fusion.8
  151.4 2.4 bitcast_dynamic-update-slice_fusion.8
  154.5 2.4 bitcast_dynamic-update-slice_fusion.8
  157.6 2.4 bitcast_dynamic-update-slice_fusion.8
  160.7 2.4 bitcast_dynamic-update-slice_fusion.8
  163.8 2.4 bitcast_dynamic-update-slice_fusion.8
  166.9 2.4 bitcast_dynamic-update-slice_fusion.8
  170.4 4.9 %all-to-all-start.1 = ((bf16[8,1,2,2,128,128]{5,4,3,2,1,0:T(8,128)(2,1)}), bf16[8,1,2,2,128,128]{5,4,3,2,1,0:T(8,128)(2,1)S(1)}, u32[]{:S(2)}, u32[]{:S(2)}) async-start(bf16[8,1,2,2,128,128]{5,4,3,2,1,0:T(8,128)(2,1)} %bitcast_select_fusion.3), calls=%async_computation.1 | async-start | bytes 2097152 | tf_op jit(solution)/shard_map/all_to_all | solution.py:151
  175.6 24.6 %while.5 = (s32[]{:T(128)}, bf16[2,2,384,384]{3,2,1,0:T(8,128)(2,1)}, s32[8,4]{0,1:T(4,128)S(1)}, bf16[8,2,2,128,128]{4,3,2,1,0:T(8,128)(2,1)S(1)}, s32[]{:T(128)}) while((s32[]{:T(128)}, bf16[2,2,384,384]{3,2,1,0:T(8,128)(2,1)}, s32[8,4]{0,1:T(4,128)S(1)}, bf16[8,2,2,128,128]{4,3,2,1,0:T(8,128)(2,1)S(1)}, s32[]{:T(128)}) %tuple.105), condition=%wide.while_cond.1, body=%wide.while_body.1.sunk | while | flops 2 | bytes 262269 | solution.py:93
  176.2 2.4 bitcast_dynamic-update-slice_fusion.9
  179.3 2.4 bitcast_dynamic-update-slice_fusion.9
  185.5 2.4 bitcast_dynamic-update-slice_fusion.9
  201.3 7.4 %all-to-all-start.3 = ((bf16[8,1,2,2,128,128]{5,4,3,2,1,0:T(8,128)(2,1)}), bf16[8,1,2,2,128,128]{5,4,3,2,1,0:T(8,128)(2,1)S(1)}, u32[]{:S(2)}, u32[]{:S(2)}) async-start(bf16[8,1,2,2,128,128]{5,4,3,2,1,0:T(8,128)(2,1)} %bitcast_select_fusion.2), calls=%async_computation.3 | async-start | bytes 2097152 | tf_op jit(solution)/shard_map/all_to_all | solution.py:151
  239.1 23.7 %while.6 = (s32[]{:T(128)}, bf16[2,2,384,384]{3,2,1,0:T(8,128)(2,1)}, s32[8,4]{0,1:T(4,128)S(1)}, bf16[8,2,2,128,128]{4,3,2,1,0:T(8,128)(2,1)S(1)}, s32[]{:T(128)}) while((s32[]{:T(128)}, bf16[2,2,384,384]{3,2,1,0:T(8,128)(2,1)}, s32[8,4]{0,1:T(4,128)S(1)}, bf16[8,2,2,128,128]{4,3,2,1,0:T(8,128)(2,1)S(1)}, s32[]{:T(128)}) %tuple.106), condition=%wide.while_cond.2, body=%wide.while_body.2.sunk | while | flops 2 | bytes 262269 | solution.py:93
  264.0 7.2 %all-to-all-start.5 = ((bf16[8,1,2,2,128,128]{5,4,3,2,1,0:T(8,128)(2,1)}), bf16[8,1,2,2,128,128]{5,4,3,2,1,0:T(8,128)(2,1)S(1)}, u32[]{:S(2)}, u32[]{:S(2)}) async-start(bf16[8,1,2,2,128,128]{5,4,3,2,1,0:T(8,128)(2,1)} %bitcast_select_fusion.1), calls=%async_computation.5 | async-start | bytes 2097152 | tf_op jit(solution)/shard_map/all_to_all | solution.py:151
  300.4 3.0 collective-permute-start.1
  303.7 24.0 %while.7 = (s32[]{:T(128)}, bf16[2,2,384,384]{3,2,1,0:T(8,128)(2,1)}, s32[8,4]{0,1:T(4,128)S(1)}, bf16[8,2,2,128,128]{4,3,2,1,0:T(8,128)(2,1)S(1)}, s32[]{:T(128)}) while((s32[]{:T(128)}, bf16[2,2,384,384]{3,2,1,0:T(8,128)(2,1)}, s32[8,4]{0,1:T(4,128)S(1)}, bf16[8,2,2,128,128]{4,3,2,1,0:T(8,128)(2,1)S(1)}, s32[]{:T(128)}) %tuple.107), condition=%wide.while_cond.3, body=%wide.while_body.3.sunk | while | flops 2 | bytes 262269 | solution.py:93
  328.8 7.2 %all-to-all-start.7 = ((bf16[8,1,2,2,128,128]{5,4,3,2,1,0:T(8,128)(2,1)}), bf16[8,1,2,2,128,128]{5,4,3,2,1,0:T(8,128)(2,1)S(1)}, u32[]{:S(2)}, u32[]{:S(2)}) async-start(bf16[8,1,2,2,128,128]{5,4,3,2,1,0:T(8,128)(2,1)} %bitcast_select_fusion), calls=%async_computation.7 | async-start | bytes 2097152 | tf_op jit(solution)/shard_map/all_to_all | solution.py:151
  368.1 14.9 %collective-permute-done.2 = f32[8,2,128,128]{3,2,0,1:T(8,128)} collective-permute-done((f32[8,2,128,128]{3,2,0,1:T(8,128)}, f32[8,2,128,128]{3,2,0,1:T(8,128)}, u32[]{:S(2)}, u32[]{:S(2)}) %collective-permute-start.2) | collective-permute-done | bytes 1048608 | tf_op jit(solution)/shard_map/ppermute | solution.py:14
  (286 shorter events, 210.4 us)
Async XLA Ops:
  2.6 101.9 %all-to-all-start.6 = ((s32[8,1,1]{2,1,0:T(1,128)}), s32[8,1,1]{2,1,0:T(1,128)S(1)}, u32[]{:S(2)}, u32[]{:S(2)}) async-start(s32[8,1,1]{2,1,0:T(1,128)} %stack.64), calls=%async_computation.6 | async-start | bytes 8192 | tf_op jit(solution)/shard_map/all_to_all | solution.py:147
  105.7 12.5 %all-to-all-start.4 = ((s32[8,1,1]{2,1,0:T(1,128)}), s32[8,1,1]{2,1,0:T(1,128)S(1)}, u32[]{:S(2)}, u32[]{:S(2)}) async-start(s32[8,1,1]{2,1,0:T(1,128)} %stack.60), calls=%async_computation.4 | async-start | bytes 8192 | tf_op jit(solution)/shard_map/all_to_all | solution.py:147
  119.4 10.8 %all-to-all-start.2 = ((s32[8,1,1]{2,1,0:T(1,128)}), s32[8,1,1]{2,1,0:T(1,128)S(1)}, u32[]{:S(2)}, u32[]{:S(2)}) async-start(s32[8,1,1]{2,1,0:T(1,128)} %stack.56), calls=%async_computation.2 | async-start | bytes 8192 | tf_op jit(solution)/shard_map/all_to_all | solution.py:147
  131.5 10.8 %all-to-all-start = ((s32[8,1,1]{2,1,0:T(1,128)}), s32[8,1,1]{2,1,0:T(1,128)S(1)}, u32[]{:S(2)}, u32[]{:S(2)}) async-start(s32[8,1,1]{2,1,0:T(1,128)} %stack.52), calls=%async_computation | async-start | bytes 8192 | tf_op jit(solution)/shard_map/all_to_all | solution.py:147
  170.4 30.9 %all-to-all-start.1 = ((bf16[8,1,2,2,128,128]{5,4,3,2,1,0:T(8,128)(2,1)}), bf16[8,1,2,2,128,128]{5,4,3,2,1,0:T(8,128)(2,1)S(1)}, u32[]{:S(2)}, u32[]{:S(2)}) async-start(bf16[8,1,2,2,128,128]{5,4,3,2,1,0:T(8,128)(2,1)} %bitcast_select_fusion.3), calls=%async_computation.1 | async-start | bytes 2097152 | tf_op jit(solution)/shard_map/all_to_all | solution.py:151
  201.3 7.4 %copy-start = (bf16[8,1,2,2,128,128]{5,4,3,2,1,0:T(8,128)(2,1)}, bf16[8,1,2,2,128,128]{5,4,3,2,1,0:T(8,128)(2,1)S(1)}, u32[]{:S(2)}) copy-start(bf16[8,1,2,2,128,128]{5,4,3,2,1,0:T(8,128)(2,1)S(1)} %all-to-all-done.1) | copy-start | bytes 3145732
  201.3 62.7 %all-to-all-start.3 = ((bf16[8,1,2,2,128,128]{5,4,3,2,1,0:T(8,128)(2,1)}), bf16[8,1,2,2,128,128]{5,4,3,2,1,0:T(8,128)(2,1)S(1)}, u32[]{:S(2)}, u32[]{:S(2)}) async-start(bf16[8,1,2,2,128,128]{5,4,3,2,1,0:T(8,128)(2,1)} %bitcast_select_fusion.2), calls=%async_computation.3 | async-start | bytes 2097152 | tf_op jit(solution)/shard_map/all_to_all | solution.py:151
  237.0 35.2 %collective-permute-start = (f32[8,2,128,128]{3,2,0,1:T(8,128)}, f32[8,2,128,128]{3,2,0,1:T(8,128)}, u32[]{:S(2)}, u32[]{:S(2)}) collective-permute-start(f32[8,2,128,128]{3,2,0,1:T(8,128)} %pad_maximum_fusion), channel_id=1, source_target_pairs={{0,8},{8,16},{16,24},{24,32},{32,40},{40,48},{48,56},{56,64},{64,7... | collective-permute-start | bytes 3145736 | tf_op jit(solution)/shard_map/ppermute | solution.py:14
  264.0 64.8 %all-to-all-start.5 = ((bf16[8,1,2,2,128,128]{5,4,3,2,1,0:T(8,128)(2,1)}), bf16[8,1,2,2,128,128]{5,4,3,2,1,0:T(8,128)(2,1)S(1)}, u32[]{:S(2)}, u32[]{:S(2)}) async-start(bf16[8,1,2,2,128,128]{5,4,3,2,1,0:T(8,128)(2,1)} %bitcast_select_fusion.1), calls=%async_computation.5 | async-start | bytes 2097152 | tf_op jit(solution)/shard_map/all_to_all | solution.py:151
  272.0 0.9 copy-start.1
  300.4 36.6 %collective-permute-start.1 = (f32[8,2,128,128]{3,2,0,1:T(8,128)}, f32[8,2,128,128]{3,2,0,1:T(8,128)}, u32[]{:S(2)}, u32[]{:S(2)}) collective-permute-start(f32[8,2,128,128]{3,2,0,1:T(8,128)} %pad_maximum_fusion.1), channel_id=1, source_target_pairs={{0,8},{8,16},{16,24},{24,32},{32,40},{40,48},{48,56},{56,64},{64,7... | collective-permute-start | bytes 3145736 | tf_op jit(solution)/shard_map/ppermute | solution.py:14
  328.8 38.4 %all-to-all-start.7 = ((bf16[8,1,2,2,128,128]{5,4,3,2,1,0:T(8,128)(2,1)}), bf16[8,1,2,2,128,128]{5,4,3,2,1,0:T(8,128)(2,1)S(1)}, u32[]{:S(2)}, u32[]{:S(2)}) async-start(bf16[8,1,2,2,128,128]{5,4,3,2,1,0:T(8,128)(2,1)} %bitcast_select_fusion), calls=%async_computation.7 | async-start | bytes 2097152 | tf_op jit(solution)/shard_map/all_to_all | solution.py:151
  364.5 18.5 %collective-permute-start.2 = (f32[8,2,128,128]{3,2,0,1:T(8,128)}, f32[8,2,128,128]{3,2,0,1:T(8,128)}, u32[]{:S(2)}, u32[]{:S(2)}) collective-permute-start(f32[8,2,128,128]{3,2,0,1:T(8,128)} %pad_maximum_fusion.2), channel_id=1, source_target_pairs={{0,8},{8,16},{16,24},{24,32},{32,40},{40,48},{48,56},{56,64},{64,7... | collective-permute-start | bytes 3145736 | tf_op jit(solution)/shard_map/ppermute | solution.py:14
